TPU v7x, 32 devices: a whole 2x2x4 slice. The times are simulated.
32 devices in a mesh: groups: 2 (over y), inst: 4 (over z), tp: 4 (over x, core).
Axes of the slice: x: 2, y: 2, z: 4, core: 2. Of those that a mesh axis runs over, the one named last changes fastest.
Arguments:
- token_hidden_input: bfloat16 [512, 8192], P(('groups', 'inst'), 'tp'), parts along dimension 0, may hold values from -6 to 6
- base_query_rows: bfloat16 [512, 8192], P(('groups', 'inst'), 'tp'), parts along dimension 0, may hold values from -5 to 5
- token_key: bfloat16 [512, 1024], P(('groups', 'inst'), 'tp'), parts along dimension 0, may hold values from -5 to 5
- token_value: bfloat16 [512, 1024], P(('groups', 'inst'), 'tp'), parts along dimension 0, may hold values from -5 to 5
- cached_key_rows: bfloat16 [512, 8, 64, 128], P(('groups', 'inst'), 'tp'), parts along dimension 0, may hold values from -5 to 5
- cached_value_rows: bfloat16 [512, 8, 64, 128], P(('groups', 'inst'), 'tp'), parts along dimension 0, may hold values from -5 to 5
- request_cache_length: int32 [512], P(('groups', 'inst')), parts along dimension 0, may hold values from 1 to 64, as said below
- request_adapter: int32 [512], P(('groups', 'inst')), parts along dimension 0, may hold values from 0 to 31, as said below
- adapter_storage_row: int32 [64], P('groups'), parts along dimension 0, may hold values from 0 to 31, as said below
- adapter_down_weight: bfloat16 [64, 8192, 64], P(('groups', 'inst'), 'tp'), parts along dimension 0, may hold values from -0.0625 to 0.0625
- adapter_up_weight: bfloat16 [64, 64, 8192], P(('groups', 'inst'), None, 'tp'), parts along dimension 0, may hold values from -0.75 to 0.75
Outputs:
- attended: bfloat16 [512, 8192], P(('groups', 'inst'), 'tp'), parts along dimension 0
There are 2 independent parts, one for each index of `groups`. A program takes and returns all parts, laid end to end along the dimension named above; each array names one. Nothing has to cross between parts.
Inputs may be any that keep to these rules, and one draw needn't show every extreme that they name: `adapter_storage_row`: storage row s lies on instance s // 8 as row s % 8 there; every row is named once. `request_adapter`: in each aligned block of 64 requests (one instance's), at most 32 requests have their adapter's storage row on one instance, and exactly 32 do for some instance. `request_cache_length`: some request has exactly 64 filled slots.
All inputs are finite; a program needn't handle non-finite values.
Results may differ from a plain program's by a relative error of at most 0.0066.
Values may be sent and summed in bfloat16 or wider, within the bound.
A program may use at most 64 MiB of HBM per device.

v0:
```python
import jax
import jax.numpy as jnp
from jax import lax
from jax.sharding import PartitionSpec as P


def body(
    token_hidden_input,
    base_query_rows,
    token_key,
    token_value,
    cached_key_rows,
    cached_value_rows,
    request_cache_length,
    request_adapter,
    adapter_storage_row,
    adapter_down_weight,
    adapter_up_weight,
):
    requests = token_hidden_input.shape[0]
    kept_blocks = adapter_down_weight.shape[0]
    owners = lax.axis_size("inst")
    capacity = max(2, 2 * requests // owners)
    catalog = adapter_storage_row.shape[0]
    matching = request_adapter[:, None] == jnp.arange(catalog, dtype=jnp.int32)[None, :]
    slot = jnp.sum(jnp.where(matching, adapter_storage_row[None, :], 0), axis=1)
    home = slot // kept_blocks
    local = slot % kept_blocks
    order = jnp.arange(requests, dtype=jnp.int32)
    earlier = (home[:, None] == home[None, :]) & (order[None, :] < order[:, None])
    rank = jnp.sum(earlier.astype(jnp.int32), axis=1)
    owner_ids = jnp.arange(owners, dtype=jnp.int32)
    places = jnp.arange(capacity, dtype=jnp.int32)
    placing = (
        (home[None, None, :] == owner_ids[:, None, None])
        & (rank[None, None, :] == places[None, :, None])
    ).astype(jnp.bfloat16)
    packed = jnp.einsum(
        "hcr,rd->hcd", placing, token_hidden_input, preferred_element_type=jnp.float32
    ).astype(jnp.bfloat16)
    labels = jnp.einsum(
        "hcr,r->hc", placing, (local + 1).astype(jnp.bfloat16), preferred_element_type=jnp.float32
    ).astype(jnp.bfloat16)
    arrived_rows, tags = (
        lax.all_to_all(packed, "inst", split_axis=0, concat_axis=0, tiled=True),
        lax.all_to_all(labels, "inst", split_axis=0, concat_axis=0, tiled=True),
    )
    which = (
        tags.astype(jnp.float32)[None, :, :]
        == (jnp.arange(kept_blocks, dtype=jnp.float32) + 1.0)[:, None, None]
    )
    partial_value = jnp.einsum(
        "alo,kog->kalg", arrived_rows, adapter_down_weight, preferred_element_type=jnp.float32
    )
    partial_value = jnp.sum(jnp.where(which[..., None], partial_value, 0.0), axis=0)
    low = lax.psum(partial_value, "tp").astype(jnp.bfloat16)
    scattered_rows = jnp.where(which[..., None], low[None], jnp.zeros((), jnp.bfloat16))
    query_update = jnp.einsum(
        "difw,dwb->ifb", scattered_rows, adapter_up_weight, preferred_element_type=jnp.float32
    ).astype(jnp.bfloat16)
    returned = lax.all_to_all(query_update, "inst", split_axis=0, concat_axis=0, tiled=True)
    correction = jnp.einsum("hcr,hcq->rq", placing, returned, preferred_element_type=jnp.float32)
    query = (base_query_rows.astype(jnp.float32) + correction).astype(jnp.bfloat16)
    kv_here = cached_key_rows.shape[1]
    length = cached_key_rows.shape[2]
    head_size = cached_key_rows.shape[3]
    group = query.shape[1] // head_size // kv_here
    scale = head_size ** (-0.5)
    q_heads = query.reshape(requests, kv_here, group, head_size)
    scores = (
        jnp.einsum("rgjh,rglh->rgjl", q_heads, cached_key_rows, preferred_element_type=jnp.float32)
        * scale
    )
    valid = jnp.arange(length, dtype=jnp.int32)[None, :] < request_cache_length[:, None]
    scores = jnp.where(valid[:, None, None, :], scores, -1e30)
    fresh_key = token_key.reshape(requests, kv_here, head_size)
    fresh = (
        jnp.einsum("rgjh,rgh->rgj", q_heads, fresh_key, preferred_element_type=jnp.float32) * scale
    )
    top = jnp.maximum(jnp.max(scores, axis=-1), fresh)
    expo = jnp.exp(scores - top[..., None])
    expo_new = jnp.exp(fresh - top)
    total = jnp.sum(expo, axis=-1) + expo_new
    weights = (expo / total[..., None]).astype(jnp.bfloat16)
    weight_new = (expo_new / total).astype(jnp.bfloat16)
    mixed = jnp.einsum(
        "rgjl,rglh->rgjh", weights, cached_value_rows, preferred_element_type=jnp.float32
    )
    fresh_value = token_value.reshape(requests, kv_here, head_size).astype(jnp.float32)
    mixed = mixed + weight_new.astype(jnp.float32)[..., None] * fresh_value[:, :, None, :]
    return mixed.reshape(requests, kv_here * group * head_size).astype(jnp.bfloat16)


def solution(mesh):
    in_specs = (
        P(("groups", "inst"), "tp"),
        P(("groups", "inst"), "tp"),
        P(("groups", "inst"), "tp"),
        P(("groups", "inst"), "tp"),
        P(("groups", "inst"), "tp", None, None),
        P(("groups", "inst"), "tp", None, None),
        P(("groups", "inst")),
        P(("groups", "inst")),
        P("groups"),
        P(("groups", "inst"), "tp", None),
        P(("groups", "inst"), None, "tp"),
    )
    out_specs = P(("groups", "inst"), "tp")
    return jax.shard_map(body, mesh=mesh, in_specs=in_specs, out_specs=out_specs, check_vma=False)
```

profile of v0, /device:TPU:0, one launch (start us, length us, event | category | flops | bytes accessed | tf_op | source)
XLA Modules:
  0.0 71.6 jit_solution(17706562561524481278)
XLA Ops:
  0.0 0.9 %select_reduce_fusion = s32[64]{0:T(128)S(1)} fusion(s32[32]{0:T(128)} %param.19, s32[64]{0:T(128)} %param.18), kind=kLoop, calls=%fused_computation.44 | loop fusion | flops 6080 | bytes 640 | tf_op jit(solution)/shard_map/reduce_sum | solution.py:26
  0.9 0.2 convert_reduce_fusion
  1.1 0.1 fusion.29
  1.3 0.6 copy.18
  1.9 6.3 %all-to-all-start = ((bf16[4,1,32]{2,1,0:T(2,128)(2,1)}), bf16[4,1,32]{2,1,0:T(2,128)(2,1)S(1)}, u32[]{:S(2)}, u32[]{:S(2)}) async-start(bf16[4,1,32]{2,1,0:T(2,128)(2,1)} %copy.18), calls=%async_computation | async-start | bytes 4096 | tf_op jit(solution)/shard_map/all_to_all | solution.py:46
  8.2 2.0 %convolution_convert_fusion = bf16[4,32,2048]{2,1,0:T(8,128)(2,1)} fusion(bf16[64,2048]{1,0:T(8,128)(2,1)} %param.11, pred[32,64]{1,0:T(8,128)(4,1)S(1)} %iota_compare_fusion.2, pred[4,64]{1,0:T(4,128)(4,1)S(1)} %iota_compare_fusion.4), kind=kOutput, calls=%fused_computation.2 | convolution fusion | flops 33824768 | bytes 788736 | tf_op jit(solution)/shard_map/hcr,rd->hcd/dot_general | solution.py:38
  10.2 3.4 %all-to-all-done = bf16[4,1,32]{2,1,0:T(2,128)(2,1)S(1)} async-done(((bf16[4,1,32]{2,1,0:T(2,128)(2,1)}), bf16[4,1,32]{2,1,0:T(2,128)(2,1)S(1)}, u32[]{:S(2)}, u32[]{:S(2)}) %all-to-all-start) | async-done | bytes 288 | tf_op jit(solution)/shard_map/all_to_all | solution.py:46
  13.7 3.5 %all-to-all-start.1 = ((bf16[4,32,2048]{2,1,0:T(8,128)(2,1)}), bf16[4,32,2048]{2,1,0:T(8,128)(2,1)S(1)}, u32[]{:S(2)}, u32[]{:S(2)}) async-start(bf16[4,32,2048]{2,1,0:T(8,128)(2,1)} %convolution_convert_fusion), calls=%async_computation.1 | async-start | bytes 1048576 | tf_op jit(solution)/shard_map/all_to_all | solution.py:45
  17.2 0.1 broadcast_compare_fusion
  17.3 13.2 %all-to-all-done.1 = bf16[4,32,2048]{2,1,0:T(8,128)(2,1)S(1)} async-done(((bf16[4,32,2048]{2,1,0:T(8,128)(2,1)}), bf16[4,32,2048]{2,1,0:T(8,128)(2,1)S(1)}, u32[]{:S(2)}, u32[]{:S(2)}) %all-to-all-start.1) | async-done | bytes 524320 | tf_op jit(solution)/shard_map/all_to_all | solution.py:45
  30.5 2.8 %fusion.14 = f32[4,32,64]{2,1,0:T(8,128)S(1)} fusion(bf16[8,2048,64]{1,2,0:T(8,128)(2,1)} %param.20, bf16[4,32,2048]{2,1,0:T(8,128)(2,1)S(1)} %all-to-all-done.1, pred[8,4,32]{2,1,0:T(4,128)(4,1)S(1)} %broadcast_compare_fusion), kind=kOutput, calls=%fused_computation.15 | convolution fusion | flops 268558336 | bytes 2655232 | tf_op jit(solution)/shard_map/alo,kog->kalg/dot_general | solution.py:52
  33.3 10.7 %psum.7 = bf16[4,32,64]{2,1,0:T(8,128)(2,1)S(1)} all-reduce(f32[4,32,64]{2,1,0:T(8,128)S(1)} %fusion.14), channel_id=1, replica_groups=mesh['groups'=2,'inst'=4,'tp'=4] {'tp'}, use_global_device_ids=true, to_apply=%region_3.4 | all-reduce | flops 8192 | bytes 49152 | tf_op jit(solution)/shard_map/psum | solution.py:56
  44.0 1.4 %fusion = bf16[4,32,2048]{2,1,0:T(8,128)(2,1)} fusion(bf16[8,64,2048]{2,1,0:T(8,128)(2,1)S(1)} %copy-done, pred[8,4,32]{2,1,0:T(4,128)(4,1)S(1)} %broadcast_compare_fusion, bf16[4,32,64]{2,1,0:T(8,128)(2,1)S(1)} %psum.7), kind=kOutput, calls=%fused_computation.1 | convolution fusion | flops 268763136 | bytes 2638848 | tf_op jit(solution)/shard_map/difw,dwb->ifb/dot_general | solution.py:58
  45.4 3.5 %all-to-all-start.2 = ((bf16[4,32,2048]{2,1,0:T(8,128)(2,1)}), bf16[4,32,2048]{2,1,0:T(8,128)(2,1)S(1)}, u32[]{:S(2)}, u32[]{:S(2)}) async-start(bf16[4,32,2048]{2,1,0:T(8,128)(2,1)} %fusion), calls=%async_computation.2 | async-start | bytes 1048576 | tf_op jit(solution)/shard_map/all_to_all | solution.py:61
  49.1 14.9 %all-to-all-done.2 = bf16[4,32,2048]{2,1,0:T(8,128)(2,1)S(1)} async-done(((bf16[4,32,2048]{2,1,0:T(8,128)(2,1)}), bf16[4,32,2048]{2,1,0:T(8,128)(2,1)S(1)}, u32[]{:S(2)}, u32[]{:S(2)}) %all-to-all-start.2) | async-done | bytes 524320 | tf_op jit(solution)/shard_map/all_to_all | solution.py:61
  64.0 0.3 fusion.17
  64.3 2.9 %fusion.52 = (f32[64,2,8]{2,1,0:T(2,128)S(1)}, f32[64,2,8,64]{3,2,1,0:T(8,128)S(1)}) fusion(bf16[64,2,8,128]{3,2,1,0:T(8,128)(2,1)S(1)} %bitcast.79, bf16[64,2,64,128]{3,2,1,0:T(8,128)(2,1)} %param.15, pred[64,64]{1,0:T(8,128)(4,1)S(1)} %iota_compare_fusion.1), kind=kOutput, calls=%fused_computation.71 | convolution fusion | flops 16972800 | bytes 2629632 | tf_op jit(solution)/shard_map/rgjh,rglh->rgjl/dot_general | solution.py:71
  67.3 0.3 fusion.53
  67.6 0.1 copy.20
  67.8 0.4 fusion.19
  68.3 0.1 copy.22
  68.4 0.1 copy.23
  68.5 2.3 %fusion.13 = bf16[64,2,8,128]{3,2,1,0:T(8,128)(2,1)S(1)} fusion(bf16[64,2,64,128]{3,2,1,0:T(8,128)(2,1)} %param.16, f32[64,2,8,64]{3,2,1,0:T(8,128)S(1)} %get-tuple-element.8, f32[64,2,128]{2,1,0:T(2,128)S(1)} %reshape.154, f32[64,2,8]{2,1,0:T(2,128)S(1)} %copy.23, f32[64,2,8]{2,1,0:T(2,128)S(1)} %copy.22, f32[64,2,8]{2,1,0:T(2,128)S(1)} %copy.20), kind=kOutput, calls=%fused_computation.14 | convolution fusion | flops 17367040 | bytes 2699264 | tf_op jit(solution)/shard_map/rgjl,rglh->rgjh/dot_general | solution.py:86
  70.9 0.8 %copy.32 = bf16[8,8,16,128]{3,1,2,0:T(8,128)(2,1)} copy(bf16[8,8,16,128]{3,2,1,0:T(8,128)(2,1)S(1)} %bitcast.81) | data formatting | bytes 524288
  (25 shorter events, 0.5 us)
Async XLA Ops:
  0.0 43.9 %copy-start = (bf16[8,64,2048]{2,1,0:T(8,128)(2,1)S(1)}, bf16[8,64,2048]{2,1,0:T(8,128)(2,1)}, u32[]{:S(2)}) copy-start(bf16[8,64,2048]{2,1,0:T(8,128)(2,1)} %param.21) | copy-start | bytes 6291460
  1.9 11.8 %all-to-all-start = ((bf16[4,1,32]{2,1,0:T(2,128)(2,1)}), bf16[4,1,32]{2,1,0:T(2,128)(2,1)S(1)}, u32[]{:S(2)}, u32[]{:S(2)}) async-start(bf16[4,1,32]{2,1,0:T(2,128)(2,1)} %copy.18), calls=%async_computation | async-start | bytes 4096 | tf_op jit(solution)/shard_map/all_to_all | solution.py:46
  13.7 16.8 %all-to-all-start.1 = ((bf16[4,32,2048]{2,1,0:T(8,128)(2,1)}), bf16[4,32,2048]{2,1,0:T(8,128)(2,1)S(1)}, u32[]{:S(2)}, u32[]{:S(2)}) async-start(bf16[4,32,2048]{2,1,0:T(8,128)(2,1)} %convolution_convert_fusion), calls=%async_computation.1 | async-start | bytes 1048576 | tf_op jit(solution)/shard_map/all_to_all | solution.py:45
  44.0 4.9 %copy-start.2 = (bf16[64,256]{1,0:T(8,128)(2,1)S(1)}, bf16[64,256]{1,0:T(8,128)(2,1)}, u32[]{:S(2)}) copy-start(bf16[64,256]{1,0:T(8,128)(2,1)} %param.13) | copy-start | bytes 98308
  44.0 5.0 %copy-start.3 = (bf16[64,256]{1,0:T(8,128)(2,1)S(1)}, bf16[64,256]{1,0:T(8,128)(2,1)}, u32[]{:S(2)}) copy-start(bf16[64,256]{1,0:T(8,128)(2,1)} %param.14) | copy-start | bytes 98308
  44.0 5.0 %copy-start.4 = (s32[64]{0:T(128)S(1)}, s32[64]{0:T(128)}, u32[]{:S(2)}) copy-start(s32[64]{0:T(128)} %param.17) | copy-start | bytes 772
  44.0 20.0 %copy-start.1 = (bf16[64,2048]{1,0:T(8,128)(2,1)S(1)}, bf16[64,2048]{1,0:T(8,128)(2,1)}, u32[]{:S(2)}) copy-start(bf16[64,2048]{1,0:T(8,128)(2,1)} %param.12) | copy-start | bytes 786436
  45.4 18.6 %all-to-all-start.2 = ((bf16[4,32,2048]{2,1,0:T(8,128)(2,1)}), bf16[4,32,2048]{2,1,0:T(8,128)(2,1)S(1)}, u32[]{:S(2)}, u32[]{:S(2)}) async-start(bf16[4,32,2048]{2,1,0:T(8,128)(2,1)} %fusion), calls=%async_computation.2 | async-start | bytes 1048576 | tf_op jit(solution)/shard_map/all_to_all | solution.py:61
where the time goes:
time: 72.1 us; the launch traced here: 71.6 us
  waiting for transfers between devices  31.6 us (44%)
  starting transfers between devices  13.3 us (18%)
  matrix products  12.2 us (17%)
  blocking collectives  10.7 us (15%)
  local copies, waits for them, and re-layouts  2.03 us (3%)
  other arithmetic  1.73 us (2%)
    all_to_all x1, waiting for transfers between devices, body(): lax.all_to_all(query_update, 'inst', split_axis=0, concat_axis=0, tiled=T...  14.9 us
    all_to_all x1, waiting for transfers between devices, body(): lax.all_to_all(packed, 'inst', split_axis=0, concat_axis=0, tiled=True)  13.2 us
    psum x1, blocking collectives, body(): low = lax.psum(partial_value, 'tp').astype(jnp.bfloat16)  10.7 us
    all_to_all x1, starting transfers between devices, body(): lax.all_to_all(labels, 'inst', split_axis=0, concat_axis=0, tiled=True)  6.32 us
    all_to_all x1, starting transfers between devices, body(): lax.all_to_all(packed, 'inst', split_axis=0, concat_axis=0, tiled=True)  3.47 us
    all_to_all x1, starting transfers between devices, body(): lax.all_to_all(query_update, 'inst', split_axis=0, concat_axis=0, tiled=T...  3.47 us
    all_to_all x1, waiting for transfers between devices, body(): lax.all_to_all(labels, 'inst', split_axis=0, concat_axis=0, tiled=True)  3.44 us
    dot_general x1, matrix products, body(): jnp.einsum('rgjh,rglh->rgjl', q_heads, cached_key_rows, preferred_element...  2.91 us
  transfers between devices with their start and end apart: 3, of which 3 were waited for; matrix products, arithmetic and copies ran while one was open for 3% of the time, Pallas kernels for 0%

commit v1 on v0

v1 whole, which is shorter than its diff:
```python
import functools

import jax
import jax.numpy as jnp
from jax import lax
from jax.experimental import pallas as pl
from jax.experimental.pallas import tpu as pltpu
from jax.sharding import PartitionSpec as P

MESH = pl.DeviceIdType.MESH
F32 = jnp.float32
BF16 = jnp.bfloat16
TILE = 16
BLOCK = 8


def iota(shape, axis):
    return lax.broadcasted_iota(jnp.int32, shape, axis)


def to_column(row, count):
    shape = (count, row.shape[1])
    return jnp.sum(jnp.where(iota(shape, 0) == iota(shape, 1), row, 0.0), axis=1, keepdims=True)


def to_row(column):
    n = column.shape[0]
    return jnp.sum(jnp.where(iota((n, n), 0) == iota((n, n), 1), column, 0.0), axis=0, keepdims=True)


def kernel(
    owners, shards, chunks,
    adapter_ref, storage_ref, length_ref,
    x_hbm, base_hbm, tk_hbm, tv_hbm, k_hbm, v_hbm, down_hbm, up_hbm,
    out_ref,
    x, base, tk, tv, kbuf, vbuf, down, up,
    snd, arr, tag_snd, tag_arr, part, delta, ret,
    in_sem, snd_send, snd_recv, tag_send, tag_recv, part_send, part_recv, ret_send, ret_recv,
):
    me = lax.axis_index("inst")
    tp = lax.axis_index("tp")
    requests, width = x.shape
    heads = kbuf.shape[0]
    slots, head = kbuf.shape[2], kbuf.shape[3]
    span = width // heads
    group = span // head
    lanes = down.shape[0]
    rank = 64
    kept = lanes // rank
    rows = owners * TILE
    peer = lambda j: {"inst": lax.rem(me + j, owners)}
    mate = lambda j: {"tp": lax.rem(tp + j, shards)}

    loads = [pltpu.make_async_copy(x_hbm, x, in_sem.at[0])]
    loads.append(pltpu.make_async_copy(down_hbm, down, in_sem.at[1]))
    loads.append(pltpu.make_async_copy(up_hbm, up, in_sem.at[2]))
    loads.append(pltpu.make_async_copy(base_hbm, base, in_sem.at[3]))
    loads.append(pltpu.make_async_copy(tk_hbm, tk, in_sem.at[4]))
    loads.append(pltpu.make_async_copy(tv_hbm, tv, in_sem.at[5]))
    for g in range(heads):
        loads.append(pltpu.make_async_copy(k_hbm.at[:, g], kbuf.at[g], in_sem.at[6 + 2 * g]))
        loads.append(pltpu.make_async_copy(v_hbm.at[:, g], vbuf.at[g], in_sem.at[7 + 2 * g]))
    for load in loads:
        load.start()

    barrier = pltpu.get_barrier_semaphore()
    for j in range(1, owners):
        pl.semaphore_signal(barrier, inc=1, device_id=peer(j), device_id_type=MESH)
    for j in range(1, shards):
        pl.semaphore_signal(barrier, inc=1, device_id=mate(j), device_id_type=MESH)

    catalog = storage_ref.shape[1]
    adapter = to_column(adapter_ref[...].astype(F32), requests)
    stored = storage_ref[...].astype(F32)
    slot = jnp.sum(
        jnp.where(adapter == iota((requests, catalog), 1).astype(F32), stored, 0.0), axis=1, keepdims=True
    )
    home = jnp.floor((slot + 0.5) * (1.0 / kept))
    tag = slot - home * kept + 1.0
    home = home - me.astype(F32)
    home = jnp.where(home < 0.0, home + owners, home)
    home_row = to_row(home)
    square = (requests, requests)
    earlier = (home == home_row) & (iota(square, 1) < iota(square, 0))
    place = jnp.sum(jnp.where(earlier, 1.0, 0.0), axis=1, keepdims=True)
    turn = jnp.floor((place + 0.5) * (1.0 / TILE))
    spot = turn * rows + home * TILE + (place - turn * TILE)
    spot_row = to_row(spot)

    for j in range(owners):
        shape = (requests, 128)
        here = (home == float(j)) & (place == iota(shape, 1).astype(F32))
        line = jnp.sum(jnp.where(here, tag, 0.0), axis=0, keepdims=True)
        if j:
            tag_snd[j] = jnp.broadcast_to(line, (8, 128))
        else:
            tag_arr[0] = jnp.broadcast_to(line, (8, 128))

    loads[0].wait()
    own = []
    order = sorted(range(1, owners), key=lambda j: (abs(2 * j - owners), j))
    sends = []
    for c in range(chunks):
        placing = (iota((rows, requests), 0).astype(F32) + float(c * rows) == spot_row)
        packed = jnp.dot(placing.astype(F32).astype(BF16), x[...], preferred_element_type=F32).astype(BF16)
        arr[c, 0] = packed[:TILE]
        snd[c] = packed.reshape(owners, TILE, width)
        if c == 0:
            pl.semaphore_wait(barrier, owners - 1 + shards - 1)
            for j in order:
                sends.append(pltpu.make_async_remote_copy(
                    src_ref=tag_snd.at[j], dst_ref=tag_arr.at[owners - j],
                    send_sem=tag_send.at[j], recv_sem=tag_recv.at[owners - j],
                    device_id=peer(j), device_id_type=MESH))
                sends[-1].start()
        for j in order:
            sends.append(pltpu.make_async_remote_copy(
                src_ref=snd.at[c, j], dst_ref=arr.at[c, owners - j],
                send_sem=snd_send.at[c, j], recv_sem=snd_recv.at[c, owners - j],
                device_id=peer(j), device_id_type=MESH))
            sends[-1].start()

    def arrived(dst, sem, j, device):
        pltpu.make_async_remote_copy(
            src_ref=dst, dst_ref=dst, send_sem=sem, recv_sem=sem,
            device_id=device, device_id_type=MESH).wait_recv()

    half = rows // 2
    which = iota((rows, lanes), 1) // rank
    left = iota((half, 128), 1) < rank
    tags = []
    for c in range(chunks):
        if c == 0:
            for j in range(1, owners):
                arrived(tag_arr.at[j], tag_recv.at[j], j, peer(j))
            loads[1].wait()
        columns = []
        for j in range(owners):
            shape = (TILE, 128)
            match = iota(shape, 1) == iota(shape, 0) + c * TILE
            columns.append(jnp.sum(jnp.where(match, tag_arr[j, 0:1, :], 0.0), axis=1, keepdims=True))
        mine = which.astype(F32) == jnp.concatenate(columns, axis=0) - 1.0
        tags.append(mine)
        for j in range(1, owners):
            arrived(arr.at[c, j], snd_recv.at[c, j], j, peer(j))
        product = lax.dot_general(
            arr[c].reshape(rows, width), down[...], (((1,), (1,)), ((), ())), preferred_element_type=F32
        )
        product = jnp.where(mine, product, 0.0)
        folded = product[:, :128]
        for a in range(1, lanes // 128):
            folded = folded + product[:, a * 128:(a + 1) * 128]
        folded = folded + pltpu.roll(folded, rank, 1)
        part[c, 0] = jnp.where(left, folded[:half], folded[half:])
        for j in range(1, shards):
            sends.append(pltpu.make_async_remote_copy(
                src_ref=part.at[c, 0], dst_ref=part.at[c, shards - j],
                send_sem=part_send.at[c, j], recv_sem=part_recv.at[c, shards - j],
                device_id=mate(j), device_id_type=MESH))
            sends[-1].start()
        for j in range(1, shards):
            arrived(part.at[c, j], part_recv.at[c, j], j, mate(j))
        total = part[c, 0]
        for j in range(1, shards):
            total = total + part[c, j]
        turned = pltpu.roll(total, rank, 1)
        low = jnp.concatenate([jnp.where(left, total, turned), jnp.where(left, turned, total)], axis=0)
        spread = jnp.where(mine, jnp.concatenate([low] * (lanes // 128), axis=1), 0.0).astype(BF16)
        if c == 0:
            loads[2].wait()
        for g in range(heads):
            update = jnp.dot(
                spread, up[:, g * span:(g + 1) * span], preferred_element_type=F32
            ).astype(BF16)
            ret[g, c, 0] = update[:TILE]
            delta[g, c] = update.reshape(owners, TILE, span)
            for j in order:
                sends.append(pltpu.make_async_remote_copy(
                    src_ref=delta.at[g, c, j], dst_ref=ret.at[g, c, owners - j],
                    send_sem=ret_send.at[g, c, j], recv_sem=ret_recv.at[g, c, owners - j],
                    device_id=peer(j), device_id_type=MESH))
                sends[-1].start()

    scale = head ** (-0.5)
    spots = chunks * rows
    undo = (iota((requests, spots), 1).astype(F32) == spot).astype(F32).astype(BF16)
    length = to_column(length_ref[...].astype(F32), requests)
    deep = BLOCK * group
    wide = BLOCK * slots
    first = (iota((deep, 1), 0) % BLOCK) * slots
    where_slot = iota((deep, wide), 1)
    for load in loads[3:6]:
        load.wait()
    for g in range(heads):
        loads[6 + 2 * g].wait()
        loads[7 + 2 * g].wait()
        for c in range(chunks):
            for j in range(1, owners):
                arrived(ret.at[g, c, j], ret_recv.at[g, c, j], j, peer(j))
        correction = jnp.dot(undo, ret[g].reshape(spots, span), preferred_element_type=F32)
        query = (base[:, g * span:(g + 1) * span].astype(F32) + correction).astype(BF16).astype(F32)
        fresh_key = tk[:, g * head:(g + 1) * head].astype(F32)
        fresh_value = tv[:, g * head:(g + 1) * head].astype(F32)
        for pair in range(0, requests, 2 * BLOCK):
            outs = []
            for r in (pair, pair + BLOCK):
                here = slice(r, r + BLOCK)
                q = jnp.concatenate([query[here, h * head:(h + 1) * head] for h in range(group)], axis=0)
                keys = kbuf[g, here].reshape(wide, head)
                values = vbuf[g, here].reshape(wide, head)
                scores = lax.dot_general(
                    q.astype(BF16), keys, (((1,), (1,)), ((), ())), preferred_element_type=F32
                ) * scale
                last = first + jnp.concatenate([length[here]] * group, axis=0).astype(jnp.int32)
                valid = (where_slot >= first) & (where_slot < last)
                scores = jnp.where(valid, scores, -1e30)
                fresh = jnp.sum(
                    q * jnp.concatenate([fresh_key[here]] * group, axis=0), axis=1, keepdims=True
                ) * scale
                top = jnp.maximum(jnp.max(scores, axis=1, keepdims=True), fresh)
                expo = jnp.exp(scores - top)
                expo_new = jnp.exp(fresh - top)
                total = jnp.sum(expo, axis=1, keepdims=True) + expo_new
                weights = (expo / total).astype(BF16)
                weight_new = (expo_new / total).astype(BF16).astype(F32)
                mixed = jnp.dot(weights, values, preferred_element_type=F32)
                outs.append(mixed + weight_new * jnp.concatenate([fresh_value[here]] * group, axis=0))
            for h in range(group):
                piece = slice(h * BLOCK, (h + 1) * BLOCK)
                out_ref[pair:pair + 2 * BLOCK, g * span + h * head:g * span + (h + 1) * head] = (
                    jnp.concatenate([out[piece] for out in outs], axis=0).astype(BF16)
                )
    for send in sends:
        send.wait_send()


def body(owners, shards, x, base, tk, tv, k, v, lengths, adapter, storage, down, up):
    requests, width = x.shape
    heads, slots, head = k.shape[1:]
    kept, _, rank = down.shape
    capacity = max(2, 2 * requests // owners)
    chunks = -(-capacity // TILE)
    span = width // heads
    lanes = kept * rank
    down = jnp.swapaxes(down, 1, 2).reshape(lanes, width)
    up = up.reshape(lanes, width)
    small = pl.BlockSpec(memory_space=pltpu.VMEM)
    large = pl.BlockSpec(memory_space=pl.ANY)
    dma = pltpu.SemaphoreType.DMA
    return pl.pallas_call(
        functools.partial(kernel, owners, shards, chunks),
        out_shape=jax.ShapeDtypeStruct((requests, width), BF16),
        in_specs=[small] * 3 + [large] * 8,
        out_specs=pl.BlockSpec(memory_space=pltpu.VMEM),
        scratch_shapes=[
            pltpu.VMEM(x.shape, BF16),
            pltpu.VMEM(base.shape, BF16),
            pltpu.VMEM(tk.shape, BF16),
            pltpu.VMEM(tv.shape, BF16),
            pltpu.VMEM((heads, requests, slots, head), BF16),
            pltpu.VMEM((heads, requests, slots, head), BF16),
            pltpu.VMEM((lanes, width), BF16),
            pltpu.VMEM((lanes, width), BF16),
            pltpu.VMEM((chunks, owners, TILE, width), BF16),
            pltpu.VMEM((chunks, owners, TILE, width), BF16),
            pltpu.VMEM((owners, 8, 128), F32),
            pltpu.VMEM((owners, 8, 128), F32),
            pltpu.VMEM((chunks, shards, owners * TILE // 2, 128), F32),
            pltpu.VMEM((heads, chunks, owners, TILE, span), BF16),
            pltpu.VMEM((heads, chunks, owners, TILE, span), BF16),
            dma((6 + 2 * heads,)),
            dma((chunks, owners)),
            dma((chunks, owners)),
            dma((owners,)),
            dma((owners,)),
            dma((chunks, shards)),
            dma((chunks, shards)),
            dma((heads, chunks, owners)),
            dma((heads, chunks, owners)),
        ],
        compiler_params=pltpu.CompilerParams(
            collective_id=0, has_side_effects=True, vmem_limit_bytes=40 * 1024 * 1024
        ),
    )(
        adapter.reshape(1, requests), storage.reshape(1, -1), lengths.reshape(1, requests),
        x, base, tk, tv, k, v, down, up,
    )


def solution(mesh):
    rows = P(("groups", "inst"), "tp")
    cache = P(("groups", "inst"), "tp", None, None)
    in_specs = (
        rows, rows, rows, rows, cache, cache,
        P(("groups", "inst")),
        P(("groups", "inst")),
        P("groups"),
        P(("groups", "inst"), "tp", None),
        P(("groups", "inst"), None, "tp"),
    )
    step = functools.partial(body, mesh.shape["inst"], mesh.shape["tp"])
    return jax.shard_map(step, mesh=mesh, in_specs=in_specs, out_specs=rows, check_vma=False)
```

time: 72.1 us -> 51 us (0.71)
  Pallas kernels: 0 us -> 38.1 us
  waiting for transfers between devices: 31.6 us -> 0 us
  starting transfers between devices: 13.3 us -> 0 us
  matrix products: 12.2 us -> 0 us
  blocking collectives: 10.7 us -> 0 us
  local copies, waits for them, and re-layouts: 2.03 us -> 12.4 us
  other arithmetic: 1.73 us -> 0 us
    pallas_call x0 -> x1, Pallas kernels: none -> 38.1 us  [body(): pl.pallas_call(functools.partial(kernel, owners, shards, chunks), out_sha...]
    all_to_all x3 -> x0, waiting for transfers between devices: 31.6 us -> none  [the longest x1 14.9 us: body(): lax.all_to_all(query_update, 'inst', split_axis=0, concat_axis=0, tiled=T...]
    all_to_all x3 -> x0, starting transfers between devices: 13.3 us -> none  [the longest x1 6.32 us: body(): lax.all_to_all(labels, 'inst', split_axis=0, concat_axis=0, tiled=True)]
    dot_general x8 -> x0, matrix products: 12.2 us -> none  [the longest x1 2.91 us: body(): jnp.einsum('rgjh,rglh->rgjl', q_heads, cached_key_rows, preferred_element...]
    unnamed x12 -> x23, local copies, waits for them, and re-layouts: 0.84 us -> 12.4 us
    psum x1 -> x0, blocking collectives: 10.7 us -> none  [body(): low = lax.psum(partial_value, 'tp').astype(jnp.bfloat16)]
    reduce_sum x3 -> x0, other arithmetic: 1.51 us -> none  [the longest x1 0.91 us: body(): slot = jnp.sum(jnp.where(matching, adapter_storage_row[None, :], 0), axis=1)]
  transfers between devices with their start and end apart: 3 -> 0, of which waited for: 3 -> 0; matrix products, arithmetic and copies ran while one was open for 3% -> 0% of each run, Pallas kernels for 0% -> 0%
where the time goes in v1:
time: 51 us; the launch traced here: 50.6 us
  Pallas kernels  38.1 us (75%)
  local copies, waits for them, and re-layouts  12.4 us (24%)
    pallas_call x1, Pallas kernels, body(): pl.pallas_call(functools.partial(kernel, owners, shards, chunks), out_sha...  38.1 us
    unnamed x23, local copies, waits for them, and re-layouts  12.4 us

profile of v1, /device:TPU:0, one launch (start us, length us, event | category | flops | bytes accessed | tf_op | source)
XLA Modules:
  0.0 50.6 jit_solution(16077793944869941594)
XLA Ops:
  0.0 0.0 copy-start
  0.0 1.6 %copy-done = bf16[64,2,64,128]{3,2,1,0:T(8,128)(2,1)S(1)} copy-done((bf16[64,2,64,128]{3,2,1,0:T(8,128)(2,1)S(1)}, bf16[64,2,64,128]{3,2,1,0:T(8,128)(2,1)}, u32[]{:S(2)}) %copy-start) | copy-done | bytes 2097176
  1.6 0.0 copy-start.1
  1.6 1.6 %copy-done.1 = bf16[64,2,64,128]{3,2,1,0:T(8,128)(2,1)S(1)} copy-done((bf16[64,2,64,128]{3,2,1,0:T(8,128)(2,1)S(1)}, bf16[64,2,64,128]{3,2,1,0:T(8,128)(2,1)}, u32[]{:S(2)}) %copy-start.1) | copy-done | bytes 2097176
  3.2 0.0 copy-start.2
  3.2 1.6 %copy-done.2 = bf16[8,2048,64]{1,2,0:T(8,128)(2,1)S(1)} copy-done((bf16[8,2048,64]{1,2,0:T(8,128)(2,1)S(1)}, bf16[8,2048,64]{1,2,0:T(8,128)(2,1)}, u32[]{:S(2)}) %copy-start.2) | copy-done | bytes 2097176
  4.8 0.0 copy-start.3
  4.8 1.6 %copy-done.3 = bf16[8,64,2048]{2,1,0:T(8,128)(2,1)S(1)} copy-done((bf16[8,64,2048]{2,1,0:T(8,128)(2,1)S(1)}, bf16[8,64,2048]{2,1,0:T(8,128)(2,1)}, u32[]{:S(2)}) %copy-start.3) | copy-done | bytes 2097176
  6.4 0.0 copy-start.4
  6.4 0.9 %copy-done.4 = bf16[64,2048]{1,0:T(8,128)(2,1)S(1)} copy-done((bf16[64,2048]{1,0:T(8,128)(2,1)S(1)}, bf16[64,2048]{1,0:T(8,128)(2,1)}, u32[]{:S(2)}) %copy-start.4) | copy-done | bytes 262168
  7.3 0.0 copy-start.5
  7.3 0.9 %copy-done.5 = bf16[64,2048]{1,0:T(8,128)(2,1)S(1)} copy-done((bf16[64,2048]{1,0:T(8,128)(2,1)S(1)}, bf16[64,2048]{1,0:T(8,128)(2,1)}, u32[]{:S(2)}) %copy-start.5) | copy-done | bytes 262168
  8.3 0.0 copy-start.6
  8.3 0.8 %copy-done.6 = bf16[64,256]{1,0:T(8,128)(2,1)S(1)} copy-done((bf16[64,256]{1,0:T(8,128)(2,1)S(1)}, bf16[64,256]{1,0:T(8,128)(2,1)}, u32[]{:S(2)}) %copy-start.6) | copy-done | bytes 32792
  9.0 0.0 copy-start.7
  9.0 0.8 %copy-done.7 = bf16[64,256]{1,0:T(8,128)(2,1)S(1)} copy-done((bf16[64,256]{1,0:T(8,128)(2,1)S(1)}, bf16[64,256]{1,0:T(8,128)(2,1)}, u32[]{:S(2)}) %copy-start.7) | copy-done | bytes 32792
  9.8 0.0 copy-start.8
  9.8 0.7 %copy-done.8 = s32[64]{0:T(128)S(1)} copy-done((s32[64]{0:T(128)S(1)}, s32[64]{0:T(128)}, u32[]{:S(2)}) %copy-start.8) | copy-done | bytes 280
  10.4 0.0 copy-start.9
  10.4 0.7 %copy-done.9 = s32[32]{0:T(128)S(1)} copy-done((s32[32]{0:T(128)S(1)}, s32[32]{0:T(128)}, u32[]{:S(2)}) %copy-start.9) | copy-done | bytes 152
  11.1 0.0 copy-start.10
  11.1 0.7 %copy-done.10 = s32[64]{0:T(128)S(1)} copy-done((s32[64]{0:T(128)S(1)}, s32[64]{0:T(128)}, u32[]{:S(2)}) %copy-start.10) | copy-done | bytes 280
  11.8 38.1 %shard_map.109 = bf16[64,2048]{1,0:T(8,128)(2,1)S(1)} custom-call(s32[1,64]{1,0:T(1,128)S(1)} %bitcast.9, s32[1,32]{1,0:T(1,128)S(1)} %bitcast.10, s32[1,64]{1,0:T(1,128)S(1)} %bitcast.11, bf16[64,2048]{1,0:T(8,128)(2,1)S(1)} %copy-done.4, bf16[64,2048]{1,0:T(8,128)(2,1)S(1)} %copy-done.5, bf16[64,256]{1,0:T(8,128)(2,1)S(1)} %copy-done.6, ...), custom_call_target="tpu_custom_call" | custom-call | tf_op jit(solution)/shard_map/pallas_call | solution.py:250
  49.9 0.7 %copy.13 = bf16[64,2048]{1,0:T(8,128)(2,1)} copy(bf16[64,2048]{1,0:T(8,128)(2,1)S(1)} %shard_map.109) | data formatting | bytes 524288
Async XLA Ops:
  0.0 1.6 %copy-start = (bf16[64,2,64,128]{3,2,1,0:T(8,128)(2,1)S(1)}, bf16[64,2,64,128]{3,2,1,0:T(8,128)(2,1)}, u32[]{:S(2)}) copy-start(bf16[64,2,64,128]{3,2,1,0:T(8,128)(2,1)} %k_hbm.1) | copy-start | bytes 6291460
  1.6 1.6 %copy-start.1 = (bf16[64,2,64,128]{3,2,1,0:T(8,128)(2,1)S(1)}, bf16[64,2,64,128]{3,2,1,0:T(8,128)(2,1)}, u32[]{:S(2)}) copy-start(bf16[64,2,64,128]{3,2,1,0:T(8,128)(2,1)} %v_hbm.1) | copy-start | bytes 6291460
  3.2 1.6 %copy-start.2 = (bf16[8,2048,64]{1,2,0:T(8,128)(2,1)S(1)}, bf16[8,2048,64]{1,2,0:T(8,128)(2,1)}, u32[]{:S(2)}) copy-start(bf16[8,2048,64]{1,2,0:T(8,128)(2,1)} %param.20) | copy-start | bytes 6291460
  4.8 1.6 %copy-start.3 = (bf16[8,64,2048]{2,1,0:T(8,128)(2,1)S(1)}, bf16[8,64,2048]{2,1,0:T(8,128)(2,1)}, u32[]{:S(2)}) copy-start(bf16[8,64,2048]{2,1,0:T(8,128)(2,1)} %param.21) | copy-start | bytes 6291460
  6.4 0.9 %copy-start.4 = (bf16[64,2048]{1,0:T(8,128)(2,1)S(1)}, bf16[64,2048]{1,0:T(8,128)(2,1)}, u32[]{:S(2)}) copy-start(bf16[64,2048]{1,0:T(8,128)(2,1)} %x_hbm.1) | copy-start | bytes 786436
  7.3 0.9 %copy-start.5 = (bf16[64,2048]{1,0:T(8,128)(2,1)S(1)}, bf16[64,2048]{1,0:T(8,128)(2,1)}, u32[]{:S(2)}) copy-start(bf16[64,2048]{1,0:T(8,128)(2,1)} %base_hbm.1) | copy-start | bytes 786436
  8.3 0.8 %copy-start.6 = (bf16[64,256]{1,0:T(8,128)(2,1)S(1)}, bf16[64,256]{1,0:T(8,128)(2,1)}, u32[]{:S(2)}) copy-start(bf16[64,256]{1,0:T(8,128)(2,1)} %tk_hbm.1) | copy-start | bytes 98308
  9.0 0.8 %copy-start.7 = (bf16[64,256]{1,0:T(8,128)(2,1)S(1)}, bf16[64,256]{1,0:T(8,128)(2,1)}, u32[]{:S(2)}) copy-start(bf16[64,256]{1,0:T(8,128)(2,1)} %tv_hbm.1) | copy-start | bytes 98308
  9.8 0.7 %copy-start.8 = (s32[64]{0:T(128)S(1)}, s32[64]{0:T(128)}, u32[]{:S(2)}) copy-start(s32[64]{0:T(128)} %param.18) | copy-start | bytes 772
  10.4 0.7 %copy-start.9 = (s32[32]{0:T(128)S(1)}, s32[32]{0:T(128)}, u32[]{:S(2)}) copy-start(s32[32]{0:T(128)} %param.19) | copy-start | bytes 388
  11.1 0.7 %copy-start.10 = (s32[64]{0:T(128)S(1)}, s32[64]{0:T(128)}, u32[]{:S(2)}) copy-start(s32[64]{0:T(128)} %param.17) | copy-start | bytes 772

commit v2 on v1

--- a/solution.py
+++ b/solution.py
@@ -30,12 +30,12 @@
 
 def kernel(
     owners, shards, chunks,
-    adapter_ref, storage_ref, length_ref,
+    adapter_hbm, storage_hbm, length_hbm,
     x_hbm, base_hbm, tk_hbm, tv_hbm, k_hbm, v_hbm, down_hbm, up_hbm,
     out_ref,
-    x, base, tk, tv, kbuf, vbuf, down, up,
+    adapter_ref, storage_ref, length_ref, x, base, tk, tv, kbuf, vbuf, down, up,
     snd, arr, tag_snd, tag_arr, part, delta, ret,
-    in_sem, snd_send, snd_recv, tag_send, tag_recv, part_send, part_recv, ret_send, ret_recv,
+    index_sem, in_sem, snd_send, snd_recv, tag_send, tag_recv, part_send, part_recv, ret_send, ret_recv,
 ):
     me = lax.axis_index("inst")
     tp = lax.axis_index("tp")
@@ -51,6 +51,13 @@
     peer = lambda j: {"inst": lax.rem(me + j, owners)}
     mate = lambda j: {"tp": lax.rem(tp + j, shards)}
 
+    index_loads = [
+        pltpu.make_async_copy(adapter_hbm, adapter_ref, index_sem.at[0]),
+        pltpu.make_async_copy(storage_hbm, storage_ref, index_sem.at[1]),
+        pltpu.make_async_copy(length_hbm, length_ref, index_sem.at[2]),
+    ]
+    for load in index_loads:
+        load.start()
     loads = [pltpu.make_async_copy(x_hbm, x, in_sem.at[0])]
     loads.append(pltpu.make_async_copy(down_hbm, down, in_sem.at[1]))
     loads.append(pltpu.make_async_copy(up_hbm, up, in_sem.at[2]))
@@ -70,6 +77,8 @@
         pl.semaphore_signal(barrier, inc=1, device_id=mate(j), device_id_type=MESH)
 
     catalog = storage_ref.shape[1]
+    for load in index_loads:
+        load.wait()
     adapter = to_column(adapter_ref[...].astype(F32), requests)
     stored = storage_ref[...].astype(F32)
     slot = jnp.sum(
@@ -99,7 +108,7 @@
     loads[0].wait()
     own = []
     order = sorted(range(1, owners), key=lambda j: (abs(2 * j - owners), j))
-    sends = []
+    sends, row_sends = [], []
     for c in range(chunks):
         placing = (iota((rows, requests), 0).astype(F32) + float(c * rows) == spot_row)
         packed = jnp.dot(placing.astype(F32).astype(BF16), x[...], preferred_element_type=F32).astype(BF16)
@@ -113,12 +122,17 @@
                     send_sem=tag_send.at[j], recv_sem=tag_recv.at[owners - j],
                     device_id=peer(j), device_id_type=MESH))
                 sends[-1].start()
+        for send in row_sends:
+            send.wait_send()
+        row_sends = []
         for j in order:
-            sends.append(pltpu.make_async_remote_copy(
+            row_sends.append(pltpu.make_async_remote_copy(
                 src_ref=snd.at[c, j], dst_ref=arr.at[c, owners - j],
                 send_sem=snd_send.at[c, j], recv_sem=snd_recv.at[c, owners - j],
                 device_id=peer(j), device_id_type=MESH))
-            sends[-1].start()
+            row_sends[-1].start()
+
+    sends += row_sends
 
     def arrived(dst, sem, j, device):
         pltpu.make_async_remote_copy(
@@ -128,7 +142,7 @@
     half = rows // 2
     which = iota((rows, lanes), 1) // rank
     left = iota((half, 128), 1) < rank
-    tags = []
+    tags, back_sends = [], []
     for c in range(chunks):
         if c == 0:
             for j in range(1, owners):
@@ -174,12 +188,16 @@
             ).astype(BF16)
             ret[g, c, 0] = update[:TILE]
             delta[g, c] = update.reshape(owners, TILE, span)
+            if c == chunks - 1 and g:
+                for send in back_sends:
+                    send.wait_send()
+                back_sends = []
             for j in order:
-                sends.append(pltpu.make_async_remote_copy(
+                back_sends.append(pltpu.make_async_remote_copy(
                     src_ref=delta.at[g, c, j], dst_ref=ret.at[g, c, owners - j],
                     send_sem=ret_send.at[g, c, j], recv_sem=ret_recv.at[g, c, owners - j],
                     device_id=peer(j), device_id_type=MESH))
-                sends[-1].start()
+                back_sends[-1].start()
 
     scale = head ** (-0.5)
     spots = chunks * rows
@@ -187,8 +205,12 @@
     length = to_column(length_ref[...].astype(F32), requests)
     deep = BLOCK * group
     wide = BLOCK * slots
-    first = (iota((deep, 1), 0) % BLOCK) * slots
-    where_slot = iota((deep, wide), 1)
+    request = iota((deep, 1), 0) % BLOCK
+    beside = max(1, 128 // slots)
+    lane_tile = beside * slots
+    first = (request % beside) * slots
+    where_slot = iota((deep, lane_tile), 1)
+    holds = [request // beside == t for t in range(wide // lane_tile)]
     for load in loads[3:6]:
         load.wait()
     for g in range(heads):
@@ -210,10 +232,13 @@
                 values = vbuf[g, here].reshape(wide, head)
                 scores = lax.dot_general(
                     q.astype(BF16), keys, (((1,), (1,)), ((), ())), preferred_element_type=F32
-                ) * scale
+                )
                 last = first + jnp.concatenate([length[here]] * group, axis=0).astype(jnp.int32)
+                every, scores = scores, scores[:, :lane_tile]
+                for t in range(1, wide // lane_tile):
+                    scores = jnp.where(holds[t], every[:, t * lane_tile:(t + 1) * lane_tile], scores)
                 valid = (where_slot >= first) & (where_slot < last)
-                scores = jnp.where(valid, scores, -1e30)
+                scores = jnp.where(valid, scores * scale, -1e30)
                 fresh = jnp.sum(
                     q * jnp.concatenate([fresh_key[here]] * group, axis=0), axis=1, keepdims=True
                 ) * scale
@@ -221,7 +246,8 @@
                 expo = jnp.exp(scores - top)
                 expo_new = jnp.exp(fresh - top)
                 total = jnp.sum(expo, axis=1, keepdims=True) + expo_new
-                weights = (expo / total).astype(BF16)
+                weights = expo / total
+                weights = jnp.concatenate([jnp.where(hold, weights, 0.0) for hold in holds], axis=1).astype(BF16)
                 weight_new = (expo_new / total).astype(BF16).astype(F32)
                 mixed = jnp.dot(weights, values, preferred_element_type=F32)
                 outs.append(mixed + weight_new * jnp.concatenate([fresh_value[here]] * group, axis=0))
@@ -230,7 +256,7 @@
                 out_ref[pair:pair + 2 * BLOCK, g * span + h * head:g * span + (h + 1) * head] = (
                     jnp.concatenate([out[piece] for out in outs], axis=0).astype(BF16)
                 )
-    for send in sends:
+    for send in sends + back_sends:
         send.wait_send()
 
 
@@ -244,15 +270,17 @@
     lanes = kept * rank
     down = jnp.swapaxes(down, 1, 2).reshape(lanes, width)
     up = up.reshape(lanes, width)
-    small = pl.BlockSpec(memory_space=pltpu.VMEM)
-    large = pl.BlockSpec(memory_space=pl.ANY)
+    large = pl.BlockSpec(memory_space=pltpu.HBM)
     dma = pltpu.SemaphoreType.DMA
     return pl.pallas_call(
         functools.partial(kernel, owners, shards, chunks),
         out_shape=jax.ShapeDtypeStruct((requests, width), BF16),
-        in_specs=[small] * 3 + [large] * 8,
+        in_specs=[large] * 11,
         out_specs=pl.BlockSpec(memory_space=pltpu.VMEM),
         scratch_shapes=[
+            pltpu.VMEM((1, requests), jnp.int32),
+            pltpu.VMEM((1, storage.shape[0]), jnp.int32),
+            pltpu.VMEM((1, requests), jnp.int32),
             pltpu.VMEM(x.shape, BF16),
             pltpu.VMEM(base.shape, BF16),
             pltpu.VMEM(tk.shape, BF16),
@@ -268,6 +296,7 @@
             pltpu.VMEM((chunks, shards, owners * TILE // 2, 128), F32),
             pltpu.VMEM((heads, chunks, owners, TILE, span), BF16),
             pltpu.VMEM((heads, chunks, owners, TILE, span), BF16),
+            dma((3,)),
             dma((6 + 2 * heads,)),
             dma((chunks, owners)),
             dma((chunks, owners)),
@@ -279,7 +308,7 @@
             dma((heads, chunks, owners)),
         ],
         compiler_params=pltpu.CompilerParams(
-            collective_id=0, has_side_effects=True, vmem_limit_bytes=40 * 1024 * 1024
+            collective_id=0, has_side_effects=True, vmem_limit_bytes=64 * 1024 * 1024
         ),
     )(
         adapter.reshape(1, requests), storage.reshape(1, -1), lengths.reshape(1, requests),

time: 51 us -> 39.1 us (0.77)
  local copies, waits for them, and re-layouts: 12.4 us -> 1.67 us
  Pallas kernels: 38.1 us -> 37.3 us
    unnamed x23 -> x1, local copies, waits for them, and re-layouts: 12.4 us -> 1.67 us
    pallas_call x1, Pallas kernels: 38.1 us -> 37.3 us  [body(): pl.pallas_call(functools.partial(kernel, owners, shards, chunks), out_sha...]
where the time goes in v2:
time: 39.1 us; the launch traced here: 39 us
  Pallas kernels  37.3 us (95%)
  local copies, waits for them, and re-layouts  1.67 us (4%)
    pallas_call x1, Pallas kernels, body(): pl.pallas_call(functools.partial(kernel, owners, shards, chunks), out_sha...  37.3 us
    unnamed x1, local copies, waits for them, and re-layouts  1.67 us

profile of v2, /device:TPU:0, one launch (start us, length us, event | category | flops | bytes accessed | tf_op | source)
XLA Modules:
  0.0 39.0 jit_solution(5191342657956441714)
XLA Ops:
  0.0 37.3 %shard_map.109 = bf16[64,2048]{1,0:T(8,128)(2,1)} custom-call(s32[1,64]{1,0:T(1,128)} %bitcast.9, s32[1,32]{1,0:T(1,128)} %bitcast.10, s32[1,64]{1,0:T(1,128)} %bitcast.11, bf16[64,2048]{1,0:T(8,128)(2,1)} %x_hbm.1, bf16[64,2048]{1,0:T(8,128)(2,1)} %base_hbm.1, bf16[64,256]{1,0:T(8,128)(2,1)} %tk_hbm.1, bf16[64,256]{1,0:T(8,128)(2,1)} %tv_hbm.1, ...), custom_call_target="tpu_custom_call" | custom-call | tf_op jit(solution)/shard_map/pallas_call | solution.py:275
  37.3 1.7 %copy.13 = bf16[64,2048]{1,0:T(8,128)(2,1)} copy(bf16[64,2048]{1,0:T(8,128)(2,1)} %shard_map.109) | data formatting | bytes 524288

commit v3 on v2

--- a/solution.py
+++ b/solution.py
@@ -208,9 +208,23 @@
     request = iota((deep, 1), 0) % BLOCK
     beside = max(1, 128 // slots)
     lane_tile = beside * slots
-    first = (request % beside) * slots
-    where_slot = iota((deep, lane_tile), 1)
     holds = [request // beside == t for t in range(wide // lane_tile)]
+    upper = request >= BLOCK // 2
+    blocks = range(0, requests, BLOCK)
+
+    def in_rows(values):
+        return jnp.concatenate([values[r:r + BLOCK] for r in blocks for _ in range(group)], axis=0)
+
+    def beside_halves(cache, g, r):
+        middle = r + BLOCK // 2
+        return jnp.concatenate(
+            [cache[g, r:middle].reshape(-1, head), cache[g, middle:middle + BLOCK // 2].reshape(-1, head)], axis=1
+        )
+
+    first = (iota((requests * group, 1), 0) % beside) * slots
+    last = first + in_rows(length).astype(jnp.int32)
+    where_slot = iota((requests * group, lane_tile), 1)
+    valid = (where_slot >= first) & (where_slot < last)
     for load in loads[3:6]:
         load.wait()
     for g in range(heads):
@@ -223,38 +237,37 @@
         query = (base[:, g * span:(g + 1) * span].astype(F32) + correction).astype(BF16).astype(F32)
         fresh_key = tk[:, g * head:(g + 1) * head].astype(F32)
         fresh_value = tv[:, g * head:(g + 1) * head].astype(F32)
-        for pair in range(0, requests, 2 * BLOCK):
-            outs = []
-            for r in (pair, pair + BLOCK):
-                here = slice(r, r + BLOCK)
-                q = jnp.concatenate([query[here, h * head:(h + 1) * head] for h in range(group)], axis=0)
-                keys = kbuf[g, here].reshape(wide, head)
-                values = vbuf[g, here].reshape(wide, head)
-                scores = lax.dot_general(
-                    q.astype(BF16), keys, (((1,), (1,)), ((), ())), preferred_element_type=F32
-                )
-                last = first + jnp.concatenate([length[here]] * group, axis=0).astype(jnp.int32)
-                every, scores = scores, scores[:, :lane_tile]
-                for t in range(1, wide // lane_tile):
-                    scores = jnp.where(holds[t], every[:, t * lane_tile:(t + 1) * lane_tile], scores)
-                valid = (where_slot >= first) & (where_slot < last)
-                scores = jnp.where(valid, scores * scale, -1e30)
-                fresh = jnp.sum(
-                    q * jnp.concatenate([fresh_key[here]] * group, axis=0), axis=1, keepdims=True
-                ) * scale
-                top = jnp.maximum(jnp.max(scores, axis=1, keepdims=True), fresh)
-                expo = jnp.exp(scores - top)
-                expo_new = jnp.exp(fresh - top)
-                total = jnp.sum(expo, axis=1, keepdims=True) + expo_new
-                weights = expo / total
-                weights = jnp.concatenate([jnp.where(hold, weights, 0.0) for hold in holds], axis=1).astype(BF16)
-                weight_new = (expo_new / total).astype(BF16).astype(F32)
-                mixed = jnp.dot(weights, values, preferred_element_type=F32)
-                outs.append(mixed + weight_new * jnp.concatenate([fresh_value[here]] * group, axis=0))
+        queries, folded = [], []
+        for r in blocks:
+            q = jnp.concatenate([query[r:r + BLOCK, h * head:(h + 1) * head] for h in range(group)], axis=0)
+            queries.append(q)
+            every = lax.dot_general(
+                q.astype(BF16), kbuf[g, r:r + BLOCK].reshape(wide, head), (((1,), (1,)), ((), ())),
+                preferred_element_type=F32,
+            )
+            scores = every[:, :lane_tile]
+            for t in range(1, len(holds)):
+                scores = jnp.where(holds[t], every[:, t * lane_tile:(t + 1) * lane_tile], scores)
+            folded.append(scores)
+        scores = jnp.where(valid, jnp.concatenate(folded, axis=0) * scale, -1e30)
+        fresh = jnp.sum(jnp.concatenate(queries, axis=0) * in_rows(fresh_key), axis=1, keepdims=True) * scale
+        top = jnp.maximum(jnp.max(scores, axis=1, keepdims=True), fresh)
+        expo = jnp.exp(scores - top)
+        expo_new = jnp.exp(fresh - top)
+        inverse = 1.0 / (jnp.sum(expo, axis=1, keepdims=True) + expo_new)
+        weights = expo * inverse
+        added = (expo_new * inverse).astype(BF16).astype(F32) * in_rows(fresh_value)
+        outs = []
+        for i, r in enumerate(blocks):
+            here = slice(i * deep, (i + 1) * deep)
+            spread = jnp.concatenate([jnp.where(hold, weights[here], 0.0) for hold in holds], axis=1)
+            mixed = jnp.dot(spread.astype(BF16), vbuf[g, r:r + BLOCK].reshape(wide, head), preferred_element_type=F32)
+            outs.append(mixed + added[here])
+        for i in range(0, len(blocks), 2):
             for h in range(group):
                 piece = slice(h * BLOCK, (h + 1) * BLOCK)
-                out_ref[pair:pair + 2 * BLOCK, g * span + h * head:g * span + (h + 1) * head] = (
-                    jnp.concatenate([out[piece] for out in outs], axis=0).astype(BF16)
+                out_ref[blocks[i]:blocks[i] + 2 * BLOCK, g * span + h * head:g * span + (h + 1) * head] = (
+                    jnp.concatenate([outs[i][piece], outs[i + 1][piece]], axis=0).astype(BF16)
                 )
     for send in sends + back_sends:
         send.wait_send()

time: 39.1 us -> 37.2 us (0.951)
  Pallas kernels: 37.3 us -> 35.4 us
    pallas_call x1, Pallas kernels: 37.3 us -> 35.4 us  [body(): pl.pallas_call(functools.partial(kernel, owners, shards, chunks), out_sha...]
where the time goes in v3:
time: 37.2 us; the launch traced here: 37.1 us
  Pallas kernels  35.4 us (95%)
  local copies, waits for them, and re-layouts  1.67 us (4%)
    pallas_call x1, Pallas kernels, body(): pl.pallas_call(functools.partial(kernel, owners, shards, chunks), out_sha...  35.4 us
    unnamed x1, local copies, waits for them, and re-layouts  1.67 us

profile of v3, /device:TPU:0, one launch (start us, length us, event | category | flops | bytes accessed | tf_op | source)
XLA Modules:
  0.0 37.1 jit_solution(18140830141066586819)
XLA Ops:
  0.0 35.4 %shard_map.109 = bf16[64,2048]{1,0:T(8,128)(2,1)} custom-call(s32[1,64]{1,0:T(1,128)} %bitcast.9, s32[1,32]{1,0:T(1,128)} %bitcast.10, s32[1,64]{1,0:T(1,128)} %bitcast.11, bf16[64,2048]{1,0:T(8,128)(2,1)} %x_hbm.1, bf16[64,2048]{1,0:T(8,128)(2,1)} %base_hbm.1, bf16[64,256]{1,0:T(8,128)(2,1)} %tk_hbm.1, bf16[64,256]{1,0:T(8,128)(2,1)} %tv_hbm.1, ...), custom_call_target="tpu_custom_call" | custom-call | tf_op jit(solution)/shard_map/pallas_call | solution.py:288
  35.4 1.7 %copy.13 = bf16[64,2048]{1,0:T(8,128)(2,1)} copy(bf16[64,2048]{1,0:T(8,128)(2,1)} %shard_map.109) | data formatting | bytes 524288

commit v4 on v3

--- a/solution.py
+++ b/solution.py
@@ -122,10 +122,10 @@
                     send_sem=tag_send.at[j], recv_sem=tag_recv.at[owners - j],
                     device_id=peer(j), device_id_type=MESH))
                 sends[-1].start()
-        for send in row_sends:
-            send.wait_send()
-        row_sends = []
-        for j in order:
+        ahead, row_sends = row_sends, []
+        for i, j in enumerate(order):
+            if ahead:
+                ahead[i].wait_send()
             row_sends.append(pltpu.make_async_remote_copy(
                 src_ref=snd.at[c, j], dst_ref=arr.at[c, owners - j],
                 send_sem=snd_send.at[c, j], recv_sem=snd_recv.at[c, owners - j],
@@ -188,10 +188,6 @@
             ).astype(BF16)
             ret[g, c, 0] = update[:TILE]
             delta[g, c] = update.reshape(owners, TILE, span)
-            if c == chunks - 1 and g:
-                for send in back_sends:
-                    send.wait_send()
-                back_sends = []
             for j in order:
                 back_sends.append(pltpu.make_async_remote_copy(
                     src_ref=delta.at[g, c, j], dst_ref=ret.at[g, c, owners - j],

time: 37.2 us -> 36.1 us (0.970)
  Pallas kernels: 35.4 us -> 34.2 us
    pallas_call x1, Pallas kernels: 35.4 us -> 34.2 us  [body(): pl.pallas_call(functools.partial(kernel, owners, shards, chunks), out_sha...]
where the time goes in v4:
time: 36.1 us; the launch traced here: 35.9 us
  Pallas kernels  34.2 us (95%)
  local copies, waits for them, and re-layouts  1.67 us (5%)
    pallas_call x1, Pallas kernels, body(): pl.pallas_call(functools.partial(kernel, owners, shards, chunks), out_sha...  34.2 us
    unnamed x1, local copies, waits for them, and re-layouts  1.67 us

profile of v4, /device:TPU:0, one launch (start us, length us, event | category | flops | bytes accessed | tf_op | source)
XLA Modules:
  0.0 35.9 jit_solution(3527094892152566198)
XLA Ops:
  0.0 34.2 %shard_map.109 = bf16[64,2048]{1,0:T(8,128)(2,1)} custom-call(s32[1,64]{1,0:T(1,128)} %bitcast.9, s32[1,32]{1,0:T(1,128)} %bitcast.10, s32[1,64]{1,0:T(1,128)} %bitcast.11, bf16[64,2048]{1,0:T(8,128)(2,1)} %x_hbm.1, bf16[64,2048]{1,0:T(8,128)(2,1)} %base_hbm.1, bf16[64,256]{1,0:T(8,128)(2,1)} %tk_hbm.1, bf16[64,256]{1,0:T(8,128)(2,1)} %tv_hbm.1, ...), custom_call_target="tpu_custom_call" | custom-call | tf_op jit(solution)/shard_map/pallas_call | solution.py:284
  34.3 1.7 %copy.13 = bf16[64,2048]{1,0:T(8,128)(2,1)} copy(bf16[64,2048]{1,0:T(8,128)(2,1)} %shard_map.109) | data formatting | bytes 524288

commit v5 on v4

--- a/solution.py
+++ b/solution.py
@@ -139,6 +139,7 @@
             src_ref=dst, dst_ref=dst, send_sem=sem, recv_sem=sem,
             device_id=device, device_id_type=MESH).wait_recv()
 
+    pieces_of = lambda c: heads if c == chunks - 1 else 1
     half = rows // 2
     which = iota((rows, lanes), 1) // rank
     left = iota((half, 128), 1) < rank
@@ -182,15 +183,16 @@
         spread = jnp.where(mine, jnp.concatenate([low] * (lanes // 128), axis=1), 0.0).astype(BF16)
         if c == 0:
             loads[2].wait()
-        for g in range(heads):
-            update = jnp.dot(
-                spread, up[:, g * span:(g + 1) * span], preferred_element_type=F32
-            ).astype(BF16)
-            ret[g, c, 0] = update[:TILE]
-            delta[g, c] = update.reshape(owners, TILE, span)
+        pieces = pieces_of(c)
+        columns = width // pieces
+        for g in range(pieces):
+            across = slice(g * columns, (g + 1) * columns)
+            update = jnp.dot(spread, up[:, across], preferred_element_type=F32).astype(BF16)
+            ret[c, 0, :, across] = update[:TILE]
+            delta[c, :, :, across] = update.reshape(owners, TILE, columns)
             for j in order:
                 back_sends.append(pltpu.make_async_remote_copy(
-                    src_ref=delta.at[g, c, j], dst_ref=ret.at[g, c, owners - j],
+                    src_ref=delta.at[c, j, :, across], dst_ref=ret.at[c, owners - j, :, across],
                     send_sem=ret_send.at[g, c, j], recv_sem=ret_recv.at[g, c, owners - j],
                     device_id=peer(j), device_id_type=MESH))
                 back_sends[-1].start()
@@ -227,9 +229,12 @@
         loads[6 + 2 * g].wait()
         loads[7 + 2 * g].wait()
         for c in range(chunks):
-            for j in range(1, owners):
-                arrived(ret.at[g, c, j], ret_recv.at[g, c, j], j, peer(j))
-        correction = jnp.dot(undo, ret[g].reshape(spots, span), preferred_element_type=F32)
+            pieces = pieces_of(c)
+            if g < pieces:
+                across = slice(g * (width // pieces), (g + 1) * (width // pieces))
+                for j in range(1, owners):
+                    arrived(ret.at[c, j, :, across], ret_recv.at[g, c, j], j, peer(j))
+        correction = jnp.dot(undo, ret[:, :, :, g * span:(g + 1) * span].reshape(spots, span), preferred_element_type=F32)
         query = (base[:, g * span:(g + 1) * span].astype(F32) + correction).astype(BF16).astype(F32)
         fresh_key = tk[:, g * head:(g + 1) * head].astype(F32)
         fresh_value = tv[:, g * head:(g + 1) * head].astype(F32)
@@ -303,8 +308,8 @@
             pltpu.VMEM((owners, 8, 128), F32),
             pltpu.VMEM((owners, 8, 128), F32),
             pltpu.VMEM((chunks, shards, owners * TILE // 2, 128), F32),
-            pltpu.VMEM((heads, chunks, owners, TILE, span), BF16),
-            pltpu.VMEM((heads, chunks, owners, TILE, span), BF16),
+            pltpu.VMEM((chunks, owners, TILE, width), BF16),
+            pltpu.VMEM((chunks, owners, TILE, width), BF16),
             dma((3,)),
             dma((6 + 2 * heads,)),
             dma((chunks, owners)),

time: 36.1 us -> 35.9 us (level)
  no operation moved by 1% of the time
where the time goes in v5:
time: 35.9 us; the launch traced here: 35.8 us
  Pallas kernels  34.1 us (95%)
  local copies, waits for them, and re-layouts  1.67 us (5%)
    pallas_call x1, Pallas kernels, body(): pl.pallas_call(functools.partial(kernel, owners, shards, chunks), out_sha...  34.1 us
    unnamed x1, local copies, waits for them, and re-layouts  1.67 us

profile of v5, /device:TPU:0, one launch (start us, length us, event | category | flops | bytes accessed | tf_op | source)
XLA Modules:
  0.0 35.8 jit_solution(9227186446900746045)
XLA Ops:
  0.0 34.1 %shard_map.109 = bf16[64,2048]{1,0:T(8,128)(2,1)} custom-call(s32[1,64]{1,0:T(1,128)} %bitcast.9, s32[1,32]{1,0:T(1,128)} %bitcast.10, s32[1,64]{1,0:T(1,128)} %bitcast.11, bf16[64,2048]{1,0:T(8,128)(2,1)} %x_hbm.1, bf16[64,2048]{1,0:T(8,128)(2,1)} %base_hbm.1, bf16[64,256]{1,0:T(8,128)(2,1)} %tk_hbm.1, bf16[64,256]{1,0:T(8,128)(2,1)} %tv_hbm.1, ...), custom_call_target="tpu_custom_call" | custom-call | tf_op jit(solution)/shard_map/pallas_call | solution.py:289
  34.1 1.7 %copy.13 = bf16[64,2048]{1,0:T(8,128)(2,1)} copy(bf16[64,2048]{1,0:T(8,128)(2,1)} %shard_map.109) | data formatting | bytes 524288

commit v6 on v5

--- a/solution.py
+++ b/solution.py
@@ -225,17 +225,26 @@
     valid = (where_slot >= first) & (where_slot < last)
     for load in loads[3:6]:
         load.wait()
+    early = base[...].astype(F32)
+    for c in range(chunks - 1):
+        for j in range(1, owners):
+            arrived(ret.at[c, j], ret_recv.at[0, c, j], j, peer(j))
+        early = early + jnp.dot(
+            undo[:, c * rows:(c + 1) * rows], ret[c].reshape(rows, width), preferred_element_type=F32)
     for g in range(heads):
         loads[6 + 2 * g].wait()
         loads[7 + 2 * g].wait()
-        for c in range(chunks):
+        for c in range(chunks - 1, chunks):
             pieces = pieces_of(c)
             if g < pieces:
                 across = slice(g * (width // pieces), (g + 1) * (width // pieces))
                 for j in range(1, owners):
                     arrived(ret.at[c, j, :, across], ret_recv.at[g, c, j], j, peer(j))
-        correction = jnp.dot(undo, ret[:, :, :, g * span:(g + 1) * span].reshape(spots, span), preferred_element_type=F32)
-        query = (base[:, g * span:(g + 1) * span].astype(F32) + correction).astype(BF16).astype(F32)
+        fixed = early[:, g * span:(g + 1) * span]
+        correction = fixed + jnp.dot(
+            undo[:, spots - rows:], ret[chunks - 1, :, :, g * span:(g + 1) * span].reshape(rows, span),
+            preferred_element_type=F32)
+        query = correction.astype(BF16).astype(F32)
         fresh_key = tk[:, g * head:(g + 1) * head].astype(F32)
         fresh_value = tv[:, g * head:(g + 1) * head].astype(F32)
         queries, folded = [], []

time: 35.9 us -> 35.9 us (level)
  no operation moved by 1% of the time
where the time goes in v6:
time: 35.9 us; the launch traced here: 35.8 us
  Pallas kernels  34.1 us (95%)
  local copies, waits for them, and re-layouts  1.67 us (5%)
    pallas_call x1, Pallas kernels, body(): pl.pallas_call(functools.partial(kernel, owners, shards, chunks), out_sha...  34.1 us
    unnamed x1, local copies, waits for them, and re-layouts  1.67 us

profile of v6, /device:TPU:0, one launch (start us, length us, event | category | flops | bytes accessed | tf_op | source)
XLA Modules:
  0.0 35.8 jit_solution(6826313171350319168)
XLA Ops:
  0.0 34.1 %shard_map.109 = bf16[64,2048]{1,0:T(8,128)(2,1)} custom-call(s32[1,64]{1,0:T(1,128)} %bitcast.9, s32[1,32]{1,0:T(1,128)} %bitcast.10, s32[1,64]{1,0:T(1,128)} %bitcast.11, bf16[64,2048]{1,0:T(8,128)(2,1)} %x_hbm.1, bf16[64,2048]{1,0:T(8,128)(2,1)} %base_hbm.1, bf16[64,256]{1,0:T(8,128)(2,1)} %tk_hbm.1, bf16[64,256]{1,0:T(8,128)(2,1)} %tv_hbm.1, ...), custom_call_target="tpu_custom_call" | custom-call | tf_op jit(solution)/shard_map/pallas_call | solution.py:298
  34.1 1.7 %copy.13 = bf16[64,2048]{1,0:T(8,128)(2,1)} copy(bf16[64,2048]{1,0:T(8,128)(2,1)} %shard_map.109) | data formatting | bytes 524288
